TPU v7x, 32 devices: a whole 2x2x4 slice. The times are simulated.
32 devices in a mesh: ctx: 8 (over z, y), tp: 4 (over x, core).
Axes of the slice: x: 2, y: 2, z: 4, core: 2. Of those that a mesh axis runs over, the one named last changes fastest.
Arguments:
- query_base: bfloat16 [1024, 3584], P('ctx', 'tp'), may hold values from -6 to 6
- key_base: bfloat16 [1024, 3584], P('ctx', 'tp'), may hold values from -6 to 6
- value_base: bfloat16 [1024, 3584], P('ctx', 'tp'), may hold values from -6 to 6
- adapter_activation: bfloat16 [1024, 128], P('ctx'), may hold values from -6 to 6
- adapter_up_weight: bfloat16 [2, 128, 3584], P(None, None, 'tp'), may hold values from -0.5 to 0.5
- output_grad: bfloat16 [1024, 3584], P('ctx', 'tp'), may hold values from -6 to 6
- stretch_doc: int32 [16], replicated, may hold values from 3 to 15, as said below
- doc_first: int32 [16], replicated, may hold values from 0 to 15, as said below
- slot_stretch: int32 [16], replicated, may hold values from 0 to 15, as said below
Outputs:
- grad_query: bfloat16 [1024, 3584], P('ctx', 'tp')
- grad_key: bfloat16 [1024, 3584], P('ctx', 'tp')
- grad_value: bfloat16 [1024, 3584], P('ctx', 'tp')
- grad_input: bfloat16 [1024, 128], P('ctx')
- grad_adapter: float32 [2, 128, 3584], P(None, None, 'tp')
Inputs may be any that keep to these rules, and one draw needn't show every extreme that they name: stretch_doc never falls along the slab; a document covers 1 to 4 consecutive stretches, the first document exactly 4, the last stretch a document of its own; a document's id is the slab index of its last stretch. doc_first[c] is the smallest stretch index with the document id of stretch c. `slot_stretch`: each stretch is held in exactly one slot; slot s lies on ctx index s // 2; the ctx indices of each aligned group of 2 hold exactly that group's 4 consecutive stretches.
All inputs are finite; a program needn't handle non-finite values.
Results may differ from a plain program's by a relative error of at most 0.012.
The roundings to bfloat16 on the way count: a program that leaves them out, or rounds other values in their place, can miss the bound.
Values may be sent and summed in bfloat16 or wider, within the bound.
No kernel may reach another device: no remote copies, remote signals or barrier semaphores. Data moves between devices by JAX's collectives and lax.ppermute only.
A program may use at most 64 MiB of HBM per device.

v0:
```python
import jax
import jax.numpy as jnp
from jax import lax
from jax.sharding import PartitionSpec as P

HEAD_WIDTH = 224
STRETCHES_DEV = 2
GROUP_SIZE = 2


masked_fill = -1e30


def passed_along(array, axis, by):
    count = lax.axis_size(axis)
    pairs = [(i, i + by) for i in range(count) if 0 <= i + by < count]
    return lax.ppermute(array, axis, pairs)


def lookup(table, wanted):
    places = jnp.arange(table.shape[0], dtype=jnp.int32)
    return jnp.sum(jnp.where(places[None, :] == wanted[:, None], table[None, :], 0), axis=1)


def adapted(base, adapter_activation, adapter_piece):
    update = jnp.dot(adapter_activation, adapter_piece, preferred_element_type=jnp.float32)
    return (base.astype(jnp.float32) + update).astype(jnp.bfloat16)


def visibility(own_stretches, other_stretches, source_ok, stretch_doc, doc_first, stretch_len):
    own_doc = lookup(stretch_doc, own_stretches)
    own_first = lookup(doc_first, own_stretches)
    other_doc = lookup(stretch_doc, other_stretches)
    earlier = (
        (other_stretches[None, :] < own_stretches[:, None])
        & (other_stretches[None, :] >= own_first[:, None])
        & (other_doc[None, :] == own_doc[:, None])
        & source_ok
    )
    same = (other_stretches[None, :] == own_stretches[:, None]) & source_ok
    inside = jnp.arange(stretch_len, dtype=jnp.int32)
    lower = inside[:, None] >= inside[None, :]
    full = earlier[:, None, :, None] | same[:, None, :, None] & lower[None, :, None, :]
    row_count = own_stretches.shape[0] * stretch_len
    return (
        full.reshape(row_count, other_stretches.shape[0] * stretch_len),
        jnp.any(earlier | same),
    )


def masked_scores(query_heads, key_heads, visible, score_scale):
    raw = (
        jnp.einsum("qhe,khe->hqk", query_heads, key_heads, preferred_element_type=jnp.float32)
        * score_scale
    )
    return jnp.where(visible[None], raw, masked_fill)


def body(
    query_base,
    key_base,
    value_base,
    adapter_activation,
    adapter_up_weight,
    output_grad,
    stretch_doc,
    doc_first,
    slot_stretch,
):
    row_count, columns = query_base.shape
    head_local = columns // HEAD_WIDTH
    stretch_len = row_count // STRETCHES_DEV
    score_scale = HEAD_WIDTH ** (-0.5)
    ctx_count = lax.axis_size("ctx")
    device_at = lax.axis_index("ctx")

    def split_heads(values):
        return values.reshape(values.shape[0], head_local, HEAD_WIDTH)

    query = adapted(query_base, adapter_activation, adapter_up_weight[0])
    value = adapted(value_base, adapter_activation, adapter_up_weight[1])
    own_stretches = lax.dynamic_slice_in_dim(slot_stretch, device_at * STRETCHES_DEV, STRETCHES_DEV)
    offsets = [shift_by for shift_by in range(1 - GROUP_SIZE, 2 * GROUP_SIZE) if shift_by != 0]
    local_pair = jnp.stack([key_base, value])
    sources = [device_at - shift_by for shift_by in [0] + offsets]

    def receive():
        return [local_pair] + [passed_along(local_pair, "ctx", shift_by) for shift_by in offsets]

    masks = []
    for source in sources:
        source_ok = (source >= 0) & (source < ctx_count)
        other = lax.dynamic_slice_in_dim(
            slot_stretch, jnp.clip(source, 0, ctx_count - 1) * STRETCHES_DEV, STRETCHES_DEV
        )
        masks.append(
            visibility(own_stretches, other, source_ok, stretch_doc, doc_first, stretch_len)
        )
    query_heads = split_heads(query)
    grad_heads = split_heads(output_grad)
    arrived = receive()
    piece_count = len(arrived)
    peak = jnp.full((head_local, row_count), masked_fill, jnp.float32)
    norm_sum = jnp.zeros((head_local, row_count), jnp.float32)
    for place in range(piece_count):
        visible, useful = masks[place]

        def gather_stats(running, pair=arrived[place], visible=visible):
            old_peak, old_sum = running
            logits = masked_scores(query_heads, split_heads(pair[0]), visible, score_scale)
            new_peak = jnp.maximum(old_peak, jnp.max(logits, axis=2))
            weights = jnp.where(visible[None], jnp.exp(logits - new_peak[..., None]), 0.0)
            return (new_peak, old_sum * jnp.exp(old_peak - new_peak) + jnp.sum(weights, axis=2))

        peak, norm_sum = lax.cond(useful, gather_stats, lambda running: running, (peak, norm_sum))

    def probabilities(key_heads, visible):
        logits = masked_scores(query_heads, key_heads, visible, score_scale)
        return (
            jnp.where(visible[None], jnp.exp(logits - peak[..., None]), 0.0) / norm_sum[..., None]
        )

    attended = jnp.zeros((row_count, head_local, HEAD_WIDTH), jnp.float32)
    for place in range(piece_count):
        visible, useful = masks[place]

        def add_values(summed, pair=arrived[place], visible=visible):
            probs_low = probabilities(split_heads(pair[0]), visible).astype(jnp.bfloat16)
            return summed + jnp.einsum(
                "hqk,khe->qhe", probs_low, split_heads(pair[1]), preferred_element_type=jnp.float32
            )

        attended = lax.cond(useful, add_values, lambda summed: summed, attended)
    row_dot = jnp.sum(grad_heads.astype(jnp.float32) * attended, axis=2).T
    query_gradient = jnp.zeros((row_count, head_local, HEAD_WIDTH), jnp.float32)
    returned = []
    for place in range(piece_count):
        visible, useful = masks[place]

        def piece_grads(summed, pair=arrived[place], visible=visible):
            key_heads = split_heads(pair[0])
            value_heads = split_heads(pair[1])
            probs = probabilities(key_heads, visible)
            probs_low = probs.astype(jnp.bfloat16)
            grad_probs = jnp.einsum(
                "qhe,khe->hqk", grad_heads, value_heads, preferred_element_type=jnp.float32
            )
            grad_scores = (probs * (grad_probs - row_dot[..., None])).astype(jnp.bfloat16)
            summed = summed + score_scale * jnp.einsum(
                "hqk,khe->qhe", grad_scores, key_heads, preferred_element_type=jnp.float32
            )
            key_terms = score_scale * jnp.einsum(
                "hqk,qhe->khe", grad_scores, query_heads, preferred_element_type=jnp.float32
            )
            value_terms = jnp.einsum(
                "hqk,qhe->khe", probs_low, grad_heads, preferred_element_type=jnp.float32
            )
            return (summed, jnp.stack([key_terms, value_terms]).reshape(2, row_count, columns))

        def skip_piece(summed):
            return (summed, jnp.zeros((2, row_count, columns), jnp.float32))

        query_gradient, terms = lax.cond(useful, piece_grads, skip_piece, query_gradient)
        returned.append(terms)
    pair_grad = returned[0]
    for place, shift_by in enumerate(offsets):
        sent_back = passed_along(returned[place + 1].astype(jnp.bfloat16), "ctx", -shift_by)
        pair_grad = pair_grad + sent_back.astype(jnp.float32)
    grad_query = query_gradient.reshape(row_count, columns).astype(jnp.bfloat16)
    grad_key = pair_grad[0].astype(jnp.bfloat16)
    grad_value = pair_grad[1].astype(jnp.bfloat16)
    input_part = jnp.einsum(
        "tc,rc->tr", grad_query, adapter_up_weight[0], preferred_element_type=jnp.float32
    ) + jnp.einsum(
        "tc,rc->tr", grad_value, adapter_up_weight[1], preferred_element_type=jnp.float32
    )
    grad_input = lax.psum(input_part, "tp").astype(jnp.bfloat16)
    adapter_part = jnp.stack(
        [
            jnp.einsum(
                "tr,tc->rc", adapter_activation, grad_query, preferred_element_type=jnp.float32
            ),
            jnp.einsum(
                "tr,tc->rc", adapter_activation, grad_value, preferred_element_type=jnp.float32
            ),
        ]
    )
    grad_adapter = lax.psum(adapter_part, "ctx")
    return (grad_query, grad_key, grad_value, grad_input, grad_adapter)


def solution(mesh):
    return jax.shard_map(
        body,
        mesh=mesh,
        in_specs=(
            P("ctx", "tp"),
            P("ctx", "tp"),
            P("ctx", "tp"),
            P("ctx", None),
            P(None, None, "tp"),
            P("ctx", "tp"),
            P(),
            P(),
            P(),
        ),
        out_specs=(
            P("ctx", "tp"),
            P("ctx", "tp"),
            P("ctx", "tp"),
            P("ctx", None),
            P(None, None, "tp"),
        ),
        check_vma=False,
    )
```

profile of v0, /device:TPU:0, one launch (start us, length us, event | category | flops | bytes accessed | tf_op | source)
XLA Modules:
  0.0 211.6 jit_solution(12766633030053424013)
XLA Ops:
  7.9 1.3 fusion.139
  10.0 5.9 %collective-permute-start.3 = (bf16[2,128,896]{2,1,0:T(8,128)(2,1)}, bf16[2,128,896]{2,1,0:T(8,128)(2,1)S(1)}, u32[]{:S(2)}, u32[]{:S(2)}) collective-permute-start(bf16[2,128,896]{2,1,0:T(8,128)(2,1)} %pad_maximum_fusion.6), channel_id=1, source_target_pairs={{0,12},{4,16},{8,20},{12,24},{16,28},{1,13},{5,17},{9,21},{13,25},... | collective-permute-start | bytes 1376264 | tf_op jit(solution)/shard_map/ppermute | solution.py:17
  16.0 3.5 %collective-permute-start.2 = (bf16[2,128,896]{2,1,0:T(8,128)(2,1)}, bf16[2,128,896]{2,1,0:T(8,128)(2,1)S(1)}, u32[]{:S(2)}, u32[]{:S(2)}) collective-permute-start(bf16[2,128,896]{2,1,0:T(8,128)(2,1)} %pad_maximum_fusion.6), channel_id=1, source_target_pairs={{0,8},{4,12},{8,16},{12,20},{16,24},{20,28},{1,9},{5,13},{9,17},{1... | collective-permute-start | bytes 1376264 | tf_op jit(solution)/shard_map/ppermute | solution.py:17
  19.5 3.4 %collective-permute-start.1 = (bf16[2,128,896]{2,1,0:T(8,128)(2,1)}, bf16[2,128,896]{2,1,0:T(8,128)(2,1)S(1)}, u32[]{:S(2)}, u32[]{:S(2)}) collective-permute-start(bf16[2,128,896]{2,1,0:T(8,128)(2,1)} %pad_maximum_fusion.6), channel_id=1, source_target_pairs={{0,4},{4,8},{8,12},{12,16},{16,20},{20,24},{24,28},{1,5},{5,9},{9,... | collective-permute-start | bytes 1376264 | tf_op jit(solution)/shard_map/ppermute | solution.py:17
  22.9 1.3 collective-permute-start
  31.9 2.1 conditional.15
  34.0 2.5 %collective-permute-done = bf16[2,128,896]{2,1,0:T(8,128)(2,1)S(1)} collective-permute-done((bf16[2,128,896]{2,1,0:T(8,128)(2,1)}, bf16[2,128,896]{2,1,0:T(8,128)(2,1)S(1)}, u32[]{:S(2)}, u32[]{:S(2)}) %collective-permute-start) | collective-permute-done | bytes 458784 | tf_op jit(solution)/shard_map/ppermute | solution.py:17
  36.4 4.5 %conditional.16 = ((f32[4,128]{1,0:T(4,128)}, f32[4,128]{1,0:T(4,128)S(1)})) conditional(s32[]{:T(128)} %convert_element_type.133, (f32[4,128]{1,0:T(4,128)}, f32[4,128]{1,0:T(4,128)S(1)}) %conditional.15, (pred[2,64,2,64]{3,2,1,0:T(4,128)(4,1)S(1)}, bf16[2,128,896]{2,1,0:T(8,128)(2,1)S(1)}, bf16[128,4,224]{0,2,1:T(8,128)(2,1)S(1)}, ...), branch_computations={%region_16.17_spmd, %region_17.0_spmd} | conditional | flops 29754368 | bytes 2713648 | solution.py:115
  36.7 1.0 copy.96
  40.9 1.3 collective-permute-done.1
  42.3 3.4 %conditional.20 = (f32[128,4,224]{0,2,1:T(8,128)}) conditional(s32[]{:T(128)} %convert_element_type.134, () %tuple.117, (pred[2,64,2,64]{3,2,1,0:T(4,128)(4,1)S(1)}, bf16[128,896]{1,0:T(8,128)(2,1)S(1)}, bf16[128,4,224]{0,2,1:T(8,128)(2,1)S(1)}, f32[4,128]{1,0:T(4,128)}, f32[4,128]{1,0:T(4,128)S(1)}, ...), branch_computations={%region_32.33_spmd, %region_33.34_spmd} | conditional | flops 59113472 | bytes 2117640 | solution.py:133
  43.4 2.2 %convolution_bitcast_fusion = f32[128,4,224]{0,2,1:T(8,128)} fusion(bf16[128,4,224]{0,2,1:T(8,128)(2,1)S(1)} %bitcast.261, bf16[128,4,224]{0,2,1:T(8,128)(2,1)S(1)} %get-tuple-element.249, bf16[128,4,224]{0,2,1:T(8,128)(2,1)} %bitcast.262, f32[4,128]{1,0:T(4,128)S(1)} %get-tuple-element.252, f32[4,128]{1,0:T(4,128)} %get-tuple-element.251, ...), kind=kOutput, calls=%fused_computation.21 | convolution fusion | flops 59113472 | bytes 1167360 | tf_op jit(solution)/shard_map/cond/branch_1_fun/hqk,khe->qhe/dot_general | solution.py:129
  45.6 3.7 %conditional.21 = (f32[128,4,224]{0,2,1:T(8,128)}) conditional(s32[]{:T(128)} %convert_element_type.133, f32[128,4,224]{0,2,1:T(8,128)} %get-tuple-element.775, (pred[2,64,2,64]{3,2,1,0:T(4,128)(4,1)S(1)}, bf16[2,128,896]{2,1,0:T(8,128)(2,1)S(1)}, bf16[128,4,224]{0,2,1:T(8,128)(2,1)S(1)}, f32[4,128]{1,0:T(4,128)}, f32[4,128]{1,0:T(4,128)S(1)}, ...), branch_computations={%region_34.35_spmd, %region_35.36_spmd} | conditional | flops 59228160 | bytes 3493896 | solution.py:133
  46.8 2.5 %fusion.20 = f32[128,4,224]{0,2,1:T(8,128)} fusion(f32[128,4,224]{0,2,1:T(8,128)} %get-tuple-element.254, bf16[128,4,224]{0,2,1:T(8,128)(2,1)} %bitcast.254, bf16[128,4,224]{0,2,1:T(8,128)(2,1)S(1)} %get-tuple-element.256, bf16[128,4,224]{0,2,1:T(8,128)(2,1)} %bitcast.253, f32[4,128]{1,0:T(4,128)S(1)} %get-tuple-element.259, ...), kind=kOutput, calls=%fused_computation.39 | convolution fusion | flops 59228160 | bytes 1626112 | tf_op jit(solution)/shard_map/cond/branch_1_fun/hqk,khe->qhe/dot_general | solution.py:129
  49.4 1.1 multiply_reduce_fusion
  50.5 4.7 %conditional.25 = (f32[128,4,224]{0,2,1:T(8,128)S(1)}, f32[2,128,896]{2,1,0:T(8,128)}) conditional(s32[]{:T(128)} %convert_element_type.134, () %tuple.110, (pred[2,64,2,64]{3,2,1,0:T(4,128)(4,1)S(1)}, bf16[128,896]{1,0:T(8,128)(2,1)S(1)}, bf16[128,4,224]{0,2,1:T(8,128)(2,1)S(1)}, f32[4,128]{1,0:T(4,128)}, f32[4,128]{1,0:T(4,128)S(1)}, ...), branch_computations={%region_43.44_spmd, %region_44.45_spmd} | conditional | flops 147849216 | bytes 9721900 | solution.py:163
  52.8 1.2 copy.121
  54.0 1.2 fusion.84
  55.2 4.6 %conditional.26 = (f32[128,4,224]{0,2,1:T(8,128)S(1)}, bf16[2,128,896]{1,2,0:T(8,128)(2,1)S(1)}) conditional(s32[]{:T(128)} %convert_element_type.133, f32[128,4,224]{0,2,1:T(8,128)S(1)} %get-tuple-element.353, (pred[2,64,2,64]{3,2,1,0:T(4,128)(4,1)}, bf16[2,128,896]{2,1,0:T(8,128)(2,1)S(1)}, bf16[128,4,224]{0,2,1:T(8,128)(2,1)S(1)}, ...), branch_computations={%region_45.46_spmd, %region_46.47_spmd} | conditional | flops 148078592 | bytes 7034924 | solution.py:163
  55.2 1.6 broadcast_in_dim.447
  61.0 1.0 copy.115
  62.1 1.0 copy.116
  64.2 1.3 collective-permute-start.7
  65.5 1.3 collective-permute-start.6
  66.8 1.3 collective-permute-start.5
  68.1 9.7 %collective-permute-start.4 = (bf16[2,128,896]{2,1,0:T(8,128)(2,1)S(1)}, bf16[2,128,896]{2,1,0:T(8,128)(2,1)S(1)}, u32[]{:S(2)}, u32[]{:S(2)}) collective-permute-start(bf16[2,128,896]{2,1,0:T(8,128)(2,1)S(1)} %copy-done.13), channel_id=1, source_target_pairs={{0,4},{4,8},{8,12},{12,16},{16,20},{20,24},{24,28},{1,5},{5,9},{9,... | collective-permute-start | bytes 1376264 | tf_op jit(solution)/shard_map/ppermute | solution.py:17
  78.1 17.5 %collective-permute-done.7 = bf16[2,128,896]{2,1,0:T(8,128)(2,1)S(1)} collective-permute-done((bf16[2,128,896]{2,1,0:T(8,128)(2,1)}, bf16[2,128,896]{2,1,0:T(8,128)(2,1)S(1)}, u32[]{:S(2)}, u32[]{:S(2)}) %collective-permute-start.7) | collective-permute-done | bytes 458784 | tf_op jit(solution)/shard_map/ppermute | solution.py:17
  95.5 10.8 %collective-permute-done.4 = bf16[2,128,896]{2,1,0:T(8,128)(2,1)S(1)} collective-permute-done((bf16[2,128,896]{2,1,0:T(8,128)(2,1)S(1)}, bf16[2,128,896]{2,1,0:T(8,128)(2,1)S(1)}, u32[]{:S(2)}, u32[]{:S(2)}) %collective-permute-start.4) | collective-permute-done | bytes 458784 | tf_op jit(solution)/shard_map/ppermute | solution.py:17
  106.3 1.5 convert_add_fusion
  111.3 11.2 %psum.14 = bf16[128,128]{1,0:T(8,128)(2,1)} all-reduce(f32[128,128]{1,0:T(8,128)S(1)} %convolution_add_fusion.2), channel_id=1, replica_groups=mesh['ctx'=8,'tp'=4] {'tp'}, use_global_device_ids=true, to_apply=%region_53.54 | all-reduce | flops 16384 | bytes 98304 | tf_op jit(solution)/shard_map/psum | solution.py:177
  122.5 79.8 %all-reduce.2.cloned.1.call-done = f32[2,128,896]{1,2,0:T(8,128)} async-done(((f32[2,128,896]{1,2,0:T(8,128)}), f32[2,128,896]{1,2,0:T(8,128)}) %all-reduce.2.cloned.1.call-update) | async-done | bytes 917520 | tf_op jit(solution)/shard_map/psum | solution.py:188
  202.3 2.4 %copy.119 = f32[2,128,896]{2,1,0:T(8,128)} copy(f32[2,128,896]{1,2,0:T(8,128)} %all-reduce.2.cloned.1.call-done) | data formatting | bytes 1835008
  (115 shorter events, 25.1 us)
Async XLA Ops:
  7.2 0.8 copy-start
  7.2 2.0 copy-start.1
  7.2 195.1 %all-reduce.2.cloned.1.call-start = ((), (), s32[]{:S(2)}) async-start(), calls=%async_computation | async-start | bytes 1835008 | tf_op jit(solution)/shard_map/psum | solution.py:188
  9.2 15.0 %copy-start.3 = (bf16[2,128,896]{2,1,0:T(8,128)(2,1)S(1)}, bf16[2,128,896]{2,1,0:T(8,128)(2,1)}, u32[]{:S(2)}) copy-start(bf16[2,128,896]{2,1,0:T(8,128)(2,1)} %param.43) | copy-start | bytes 1376260
  9.2 15.0 %copy-start.15 = (bf16[128,896]{1,0:T(8,128)(2,1)S(1)}, bf16[128,896]{1,0:T(8,128)(2,1)}, u32[]{:S(2)}) copy-start(bf16[128,896]{1,0:T(8,128)(2,1)} %param.39) | copy-start | bytes 688132
  10.0 32.2 %collective-permute-start.3 = (bf16[2,128,896]{2,1,0:T(8,128)(2,1)}, bf16[2,128,896]{2,1,0:T(8,128)(2,1)S(1)}, u32[]{:S(2)}, u32[]{:S(2)}) collective-permute-start(bf16[2,128,896]{2,1,0:T(8,128)(2,1)} %pad_maximum_fusion.6), channel_id=1, source_target_pairs={{0,12},{4,16},{8,20},{12,24},{16,28},{1,13},{5,17},{9,21},{13,25},... | collective-permute-start | bytes 1376264 | tf_op jit(solution)/shard_map/ppermute | solution.py:17
  16.0 26.3 %collective-permute-start.2 = (bf16[2,128,896]{2,1,0:T(8,128)(2,1)}, bf16[2,128,896]{2,1,0:T(8,128)(2,1)S(1)}, u32[]{:S(2)}, u32[]{:S(2)}) collective-permute-start(bf16[2,128,896]{2,1,0:T(8,128)(2,1)} %pad_maximum_fusion.6), channel_id=1, source_target_pairs={{0,8},{4,12},{8,16},{12,20},{16,24},{20,28},{1,9},{5,13},{9,17},{1... | collective-permute-start | bytes 1376264 | tf_op jit(solution)/shard_map/ppermute | solution.py:17
  19.5 22.8 %collective-permute-start.1 = (bf16[2,128,896]{2,1,0:T(8,128)(2,1)}, bf16[2,128,896]{2,1,0:T(8,128)(2,1)S(1)}, u32[]{:S(2)}, u32[]{:S(2)}) collective-permute-start(bf16[2,128,896]{2,1,0:T(8,128)(2,1)} %pad_maximum_fusion.6), channel_id=1, source_target_pairs={{0,4},{4,8},{8,12},{12,16},{16,20},{20,24},{24,28},{1,5},{5,9},{9,... | collective-permute-start | bytes 1376264 | tf_op jit(solution)/shard_map/ppermute | solution.py:17
  22.9 13.5 %collective-permute-start = (bf16[2,128,896]{2,1,0:T(8,128)(2,1)}, bf16[2,128,896]{2,1,0:T(8,128)(2,1)S(1)}, u32[]{:S(2)}, u32[]{:S(2)}) collective-permute-start(bf16[2,128,896]{2,1,0:T(8,128)(2,1)} %pad_maximum_fusion.6), channel_id=1, source_target_pairs={{4,0},{8,4},{12,8},{16,12},{20,16},{24,20},{28,24},{5,1},{9,5},{13... | collective-permute-start | bytes 1376264 | tf_op jit(solution)/shard_map/ppermute | solution.py:17
  24.5 0.7 copy-start.16
  25.2 0.7 copy-start.18
  25.2 0.7 copy-start.19
  30.2 0.9 copy-start.14
  31.9 10.4 %copy-start.10 = (pred[2,64,2,64]{3,2,1,0:T(4,128)(4,1)}, pred[2,64,2,64]{3,2,1,0:T(4,128)(4,1)S(1)}, u32[]{:S(2)}) copy-start(pred[2,64,2,64]{3,2,1,0:T(4,128)(4,1)S(1)} %get-tuple-element.712) | copy-start | bytes 49156
  31.9 13.8 %copy-start.9 = (pred[2,64,2,64]{3,2,1,0:T(4,128)(4,1)}, pred[2,64,2,64]{3,2,1,0:T(4,128)(4,1)S(1)}, u32[]{:S(2)}) copy-start(pred[2,64,2,64]{3,2,1,0:T(4,128)(4,1)S(1)} %get-tuple-element.709) | copy-start | bytes 49156
  31.9 17.4 %copy-start.7 = (pred[2,64,2,64]{3,2,1,0:T(4,128)(4,1)}, pred[2,64,2,64]{3,2,1,0:T(4,128)(4,1)S(1)}, u32[]{:S(2)}) copy-start(pred[2,64,2,64]{3,2,1,0:T(4,128)(4,1)S(1)} %get-tuple-element.710) | copy-start | bytes 49156
  31.9 17.4 %copy-start.5 = (pred[2,64,2,64]{3,2,1,0:T(4,128)(4,1)}, pred[2,64,2,64]{3,2,1,0:T(4,128)(4,1)S(1)}, u32[]{:S(2)}) copy-start(pred[2,64,2,64]{3,2,1,0:T(4,128)(4,1)S(1)} %get-tuple-element.711) | copy-start | bytes 49156
  37.7 0.9 slice-start
  49.4 1.1 copy-start.11
  51.0 1.0 copy-start.12
  57.0 0.7 copy-start.17
  59.8 1.0 copy-start.8
  61.0 1.0 copy-start.6
  63.2 4.9 %copy-start.13 = (bf16[2,128,896]{2,1,0:T(8,128)(2,1)S(1)}, bf16[2,128,896]{2,1,0:T(8,128)(2,1)}, u32[]{:S(2)}) copy-start(bf16[2,128,896]{2,1,0:T(8,128)(2,1)} %copy.113) | copy-start | bytes 1376260
  64.2 31.3 %collective-permute-start.7 = (bf16[2,128,896]{2,1,0:T(8,128)(2,1)}, bf16[2,128,896]{2,1,0:T(8,128)(2,1)S(1)}, u32[]{:S(2)}, u32[]{:S(2)}) collective-permute-start(bf16[2,128,896]{2,1,0:T(8,128)(2,1)} %copy.117), channel_id=1, source_target_pairs={{12,0},{16,4},{20,8},{24,12},{28,16},{13,1},{17,5},{21,9},{25,13},... | collective-permute-start | bytes 1376264 | tf_op jit(solution)/shard_map/ppermute | solution.py:17
  65.5 30.0 %collective-permute-start.6 = (bf16[2,128,896]{2,1,0:T(8,128)(2,1)}, bf16[2,128,896]{2,1,0:T(8,128)(2,1)S(1)}, u32[]{:S(2)}, u32[]{:S(2)}) collective-permute-start(bf16[2,128,896]{2,1,0:T(8,128)(2,1)} %copy.116), channel_id=1, source_target_pairs={{8,0},{12,4},{16,8},{20,12},{24,16},{28,20},{9,1},{13,5},{17,9},{2... | collective-permute-start | bytes 1376264 | tf_op jit(solution)/shard_map/ppermute | solution.py:17
  66.8 28.7 %collective-permute-start.5 = (bf16[2,128,896]{2,1,0:T(8,128)(2,1)}, bf16[2,128,896]{2,1,0:T(8,128)(2,1)S(1)}, u32[]{:S(2)}, u32[]{:S(2)}) collective-permute-start(bf16[2,128,896]{2,1,0:T(8,128)(2,1)} %copy.115), channel_id=1, source_target_pairs={{4,0},{8,4},{12,8},{16,12},{20,16},{24,20},{28,24},{5,1},{9,5},{13... | collective-permute-start | bytes 1376264 | tf_op jit(solution)/shard_map/ppermute | solution.py:17
  68.1 38.2 %collective-permute-start.4 = (bf16[2,128,896]{2,1,0:T(8,128)(2,1)S(1)}, bf16[2,128,896]{2,1,0:T(8,128)(2,1)S(1)}, u32[]{:S(2)}, u32[]{:S(2)}) collective-permute-start(bf16[2,128,896]{2,1,0:T(8,128)(2,1)S(1)} %copy-done.13), channel_id=1, source_target_pairs={{0,4},{4,8},{8,12},{12,16},{16,20},{20,24},{24,28},{1,5},{5,9},{9,... | collective-permute-start | bytes 1376264 | tf_op jit(solution)/shard_map/ppermute | solution.py:17
  108.5 2.5 %copy-start.2 = (bf16[128,896]{1,0:T(8,128)(2,1)}, bf16[128,896]{1,0:T(8,128)(2,1)S(1)}, u32[]{:S(2)}) copy-start(bf16[128,896]{1,0:T(8,128)(2,1)S(1)} %get-tuple-element.706) | copy-start | bytes 688132
  109.8 1.0 copy-start.4
Sparse Core Ops, SparseCore 0:
  109.9 92.3 all-reduce.1
where the time goes:
time: 213 us; the launch traced here: 212 us
  waiting for transfers between devices  112 us (53%)
  starting transfers between devices  27.7 us (13%)
  local copies, waits for them, and re-layouts  21.2 us (10%)
  between operations  17.7 us (8%)
  matrix products  12.5 us (6%)
  blocking collectives  11.2 us (5%)
  other arithmetic  8.85 us (4%)
    psum x1, waiting for transfers between devices, body(): grad_adapter = lax.psum(adapter_part, 'ctx')  79.8 us
    ppermute x8, waiting for transfers between devices, passed_along(): return lax.ppermute(array, axis, pairs)  32.1 us
    ppermute x8, starting transfers between devices, passed_along(): return lax.ppermute(array, axis, pairs)  27.7 us
    psum x1, blocking collectives, body(): grad_input = lax.psum(input_part, 'tp').astype(jnp.bfloat16)  11.2 us
    unnamed x39, local copies, waits for them, and re-layouts  6.4 us
    cond x5, local copies, waits for them, and re-layouts, body(): lax.cond(useful, piece_grads, skip_piece, query_gradient)  5.21 us
    dot_general x2, matrix products, add_values(): jnp.einsum('hqk,khe->qhe', probs_low, split_heads(pair[1]), preferred_ele...  4.73 us
  transfers between devices with their start and end apart: 9, of which 5 were waited for; matrix products, arithmetic and copies ran while one was open for 4% of the time, Pallas kernels for 0%

commit v1 on v0

v1 whole, which is shorter than its diff:
```python
import functools

import jax
import jax.numpy as jnp
from jax import lax
from jax.experimental import pallas as pl
from jax.experimental.pallas import tpu as pltpu
from jax.sharding import PartitionSpec as P

HEAD_WIDTH = 224
STRETCHES_DEV = 2
GROUP_SIZE = 2
GROUP_STRETCHES = STRETCHES_DEV * GROUP_SIZE

masked_fill = -1e30
BF16 = jnp.bfloat16
F32 = jnp.float32


def swapped(values):
    half = values.shape[1] // 2
    return jnp.concatenate([values[:, half:], values[:, :half]], axis=1)


def dot(a, b, contract):
    return lax.dot_general(a, b, (contract, ((), ())), preferred_element_type=F32)


def call(kernel, outs, in_smem=0, flops=0):
    def run(*args):
        specs = [
            pl.BlockSpec(memory_space=pltpu.SMEM if i < in_smem else pltpu.VMEM)
            for i in range(len(args))
        ]
        moved = sum(a.size * a.dtype.itemsize for a in (*args, *outs))
        return pl.pallas_call(
            kernel,
            out_shape=outs,
            in_specs=specs,
            out_specs=[pl.BlockSpec(memory_space=pltpu.VMEM) for _ in outs],
            compiler_params=pltpu.CompilerParams(vmem_limit_bytes=40 * 1024 * 1024),
            cost_estimate=pl.CostEstimate(
                flops=flops, bytes_accessed=moved, transcendentals=0
            ),
        )(*args)

    return run


def ctx_at():
    return lax.axis_index("ctx").astype(jnp.int32)


def is_upper():
    return (ctx_at() % GROUP_SIZE) == 1


def is_even():
    return ((ctx_at() // GROUP_SIZE) % 2) == 0


def adapted(base, act, piece):
    update = jnp.dot(act, piece, preferred_element_type=F32)
    return (base.astype(F32) + update).astype(BF16).astype(F32)


def half_of(values, lower):
    half = values.shape[1] // 2
    return jnp.where(lower, values[:, :half], values[:, half:])


def head_of(values, h):
    return values[:, h * HEAD_WIDTH : (h + 1) * HEAD_WIDTH]


def put_pack(out, arrays, h, act=None):
    rows = arrays[0].shape[0]
    stretch_len = rows // STRETCHES_DEV
    pack = jnp.concatenate([head_of(values, h) for values in arrays], axis=1).astype(BF16)
    for s in range(STRETCHES_DEV):
        here = slice(s * stretch_len, (s + 1) * stretch_len)
        out[s, :, : pack.shape[1]] = pack[here]
        if act is not None:
            out[s, :, pack.shape[1] :] = act[here]


def first_kernel(
    k_hbm, v_hbm, q_hbm, g_hbm, a_hbm, w_hbm,
    out, k_ref, v_ref, q_ref, g_ref, a_ref, w_ref, sems,
):
    ends = [
        (a_hbm, a_ref), (w_hbm, w_ref), (v_hbm, v_ref), (q_hbm, q_ref), (k_hbm, k_ref),
        (g_hbm, g_ref),
    ]
    copies = [pltpu.make_async_copy(x, y, sems.at[i]) for i, (x, y) in enumerate(ends)]
    for copy in copies:
        copy.start()
    for copy in copies:
        copy.wait()
    act, lower = a_ref[...], is_upper()
    arrays = (
        k_ref[...].astype(F32),
        adapted(v_ref[...], act, w_ref[1]),
        adapted(q_ref[...], act, w_ref[0]),
        g_ref[...].astype(F32),
    )
    put_pack(out, [half_of(values, lower) for values in arrays], 0, act)


def rest_kernel(
    ctx_count, doc, first, slot, k_ref, v_ref, q_ref, g_ref, a_ref, w_ref,
    sent, own_first, own_second, w_out, places, limits,
):
    act, lower = a_ref[...], is_upper()
    arrays = (
        k_ref[...].astype(F32),
        adapted(v_ref[...], act, w_ref[1]),
        adapted(q_ref[...], act, w_ref[0]),
        g_ref[...].astype(F32),
    )
    put_pack(sent, [half_of(values, lower) for values in arrays], 1)
    mine = [half_of(values, jnp.logical_not(lower)) for values in arrays]
    put_pack(own_first, mine, 0, act)
    put_pack(own_second, mine, 1)
    maps = [half_of(w_ref[i].astype(F32), jnp.logical_not(lower)) for i in range(2)]
    for h in range(2):
        for i in range(2):
            w_out[2 * h + i] = head_of(maps[i], h).astype(BF16)
    put_tables(ctx_count, doc, first, slot, places, limits)


def put_tables(ctx_count, doc, first, slot, places, limits):
    at = ctx_at()
    stretch_len = limits.shape[1] // (GROUP_STRETCHES + 1)
    partner = at + 1 - 2 * (at % GROUP_SIZE)
    has_prev = at >= GROUP_SIZE
    has_next = at < ctx_count - GROUP_SIZE
    base = (at // GROUP_SIZE) * GROUP_STRETCHES
    mine = [
        slot[owner * STRETCHES_DEV + s] for owner in (at, partner) for s in range(STRETCHES_DEV)
    ]
    held = [c % GROUP_STRETCHES for c in mine]
    lanes = lax.broadcasted_iota(jnp.int32, (1, places.shape[1]), 1)
    for row in range(2):
        own = jnp.where(lanes < 2 * HEAD_WIDTH, held[2 * row], held[2 * row + 1])
        places[row : row + 1, :] = own
    four = jnp.where(lanes < 3 * HEAD_WIDTH, held[2], held[3])
    four = jnp.where(lanes < 2 * HEAD_WIDTH, held[1], four)
    places[2:3, :] = jnp.where(lanes < HEAD_WIDTH, held[0], four)
    for j, place in enumerate(held):
        places[3 + j : 4 + j, :] = jnp.full(lanes.shape, place, jnp.int32)
    following = jnp.where(has_next, base + GROUP_STRETCHES, base)
    third = jnp.where(has_prev, base - 2, base)
    fourth = jnp.where(has_prev, base - 1, base)
    left = [(c % GROUP_STRETCHES == 0) & (first[c] < c - 2) for c in mine + [following]]
    queries = [(c, jnp.logical_not(gone)) for c, gone in zip(mine, left)]
    queries.append((following, left[-1] & has_next))
    always = at >= 0
    keys = [(c, always) for c in mine] + [(third, has_prev), (fourth, has_prev)]
    keys.append((following, has_next))
    lanes = lax.broadcasted_iota(jnp.int32, (1, limits.shape[1]), 1)
    for j, (key, there) in enumerate(keys):
        key_doc = doc[key]
        row = jnp.full(lanes.shape, stretch_len, jnp.int32)
        for i, (query, active) in enumerate(queries):
            earlier = (key < query) & (key >= first[query]) & (key_doc == doc[query])
            limit = jnp.where(earlier, -stretch_len, jnp.where(key == query, 0, stretch_len))
            limit = jnp.where(active & there, limit, stretch_len)
            here = (lanes >= i * stretch_len) & (lanes < (i + 1) * stretch_len)
            row = jnp.where(here, limit, row)
        limits[j : j + 1, :] = row


def edge_kernel(places, own, peer, low_out, high_out):
    width = 4 * HEAD_WIDTH
    every = range(STRETCHES_DEV)
    packs = [ref[s].astype(F32) for ref in (own, peer) for s in every]

    def held(place):
        found = packs[0]
        for j in range(1, len(packs)):
            here = places[3 + j : 4 + j, : found.shape[1]] == place
            found = jnp.where(jnp.broadcast_to(here, found.shape), packs[j], found)
        return found

    start, third, fourth = held(0), held(2), held(3)
    pair = 2 * HEAD_WIDTH
    to_next = [third[:, :pair], fourth[:, :pair], third[:, width:], fourth[:, width:]]
    to_prev = [start[:, :width], start[:, width:], start[:, width:]]
    if own.shape[2] == width:
        to_next, to_prev = to_next[:2], to_prev[:1]
    to_next = jnp.concatenate(to_next, axis=1).astype(BF16)
    to_prev = jnp.concatenate(to_prev, axis=1).astype(BF16)
    low_out[...] = jnp.where(is_even(), to_next, to_prev)
    high_out[...] = jnp.where(is_even(), to_prev, to_next)


def attend_kernel(h, limits, own, peer, low_in, high_in, *rest):
    if h == 0:
        act_out, kv_own, kv_peer, dq_out, low_out, high_out, ap_out = rest
    else:
        act_in, low_first, high_first, ap_first = rest[:4]
        kv_own, kv_peer, dq_out, low_out, high_out, ap_out = rest[4:]
    stretch_len = kv_own.shape[0]
    width, pair = 4 * HEAD_WIDTH, 2 * HEAD_WIDTH
    score_scale = HEAD_WIDTH ** (-0.5)
    rows = limits.shape[1]
    inside = lax.broadcasted_iota(jnp.int32, (stretch_len, rows), 1) % stretch_len
    diff = inside - lax.broadcasted_iota(jnp.int32, (stretch_len, rows), 0)
    key_count = GROUP_STRETCHES + 3
    visible = jnp.concatenate([diff >= limits[j : j + 1, :] for j in range(key_count)], axis=0)

    from_next = jnp.where(is_even(), low_in[...], high_in[...])
    from_prev = jnp.where(is_even(), high_in[...], low_in[...])
    packs = [ref[s] for ref in (own, peer) for s in range(STRETCHES_DEV)]
    pairs = packs + [from_prev[:, :pair], from_prev[:, pair:width], from_next]

    def stacked(arrays, i):
        return jnp.concatenate([head_of(values, i) for values in arrays], axis=0)

    key, value = stacked(pairs, 0), stacked(pairs, 1)
    query, grad = stacked(packs + [from_next], 2), stacked(packs + [from_next], 3)
    if h == 0:
        rank = own.shape[2] - width
        acts = [values[:, width:] for values in packs]
        acts += [from_prev[:, width : width + rank], from_prev[:, width + rank :]]
        act = jnp.concatenate(acts + [from_next[:, width : width + rank]], axis=0)
        act_out[...] = act
    else:
        act = act_in[...]
    count = GROUP_STRETCHES * stretch_len
    act_query = jnp.concatenate([act[:count], act[-stretch_len:]], axis=0)

    scores = jnp.where(visible, dot(key, query, ((1,), (1,))) * score_scale, masked_fill)
    peak = jnp.max(scores, axis=0, keepdims=True)
    expo = jnp.where(visible, jnp.exp(scores - peak), 0.0)
    norm_sum = jnp.maximum(jnp.sum(expo, axis=0, keepdims=True), 1.0)
    probs = expo / norm_sum
    probs_low = probs.astype(BF16)
    grad_probs = dot(value, grad, ((1,), (1,)))
    row_dot = jnp.sum(probs_low.astype(F32) * grad_probs, axis=0, keepdims=True)
    grad_scores = (probs * (grad_probs - row_dot)).astype(BF16)
    dq = dot(grad_scores, key, ((0,), (0,))) * score_scale
    dk = dot(grad_scores, query, ((1,), (0,))) * score_scale
    dv = dot(probs_low, grad, ((1,), (0,)))
    ap_q = dot(act_query, dq.astype(BF16), ((0,), (0,)))
    ap_v = dot(act, dv.astype(BF16), ((0,), (0,)))

    def beside(*parts):
        return jnp.concatenate(
            [values[i * stretch_len : (i + 1) * stretch_len] for values, i in parts], axis=1
        )

    to_prev = beside((dk, 4), (dv, 4), (dk, 5), (dv, 5)).astype(BF16)
    to_next = beside((dk, 6), (dv, 6), (dq, 4), (dq, 4)).astype(BF16)
    low_back = jnp.where(is_even(), to_next, to_prev)
    high_back = jnp.where(is_even(), to_prev, to_next)
    kv_own[...] = beside((dk, 0), (dv, 0), (dk, 1), (dv, 1))
    kv_peer[...] = beside((dk, 2), (dv, 2), (dk, 3), (dv, 3))
    dq_out[...] = beside((dq, 0), (dq, 1), (dq, 2), (dq, 3)).astype(BF16)
    ap = beside((ap_q, 0), (ap_v, 0), (ap_q, 1), (ap_v, 1))
    if h == 0:
        low_out[...], high_out[...], ap_out[...] = low_back, high_back, ap
        return
    high_out[:, :width] = high_first[...]
    high_out[:, width:] = high_back
    low_out[:, :width] = low_first[...]
    low_out[:, width : 2 * width] = low_back
    low_out[:, 2 * width :] = jnp.where(is_even(), ap, ap_first[...]).astype(BF16)
    ap_out[...] = jnp.where(is_even(), ap_first[...], ap)


def put_totals(row, places, kvs, dqs, high_in, low_in, out):
    width, pair = 4 * HEAD_WIDTH, 2 * HEAD_WIDTH
    for h, (kv, dq) in enumerate(zip(kvs, dqs)):
        here = slice(h * width, (h + 1) * width)
        from_next = jnp.where(is_even(), low_in[:, here], high_in[:, here]).astype(F32)
        from_prev = jnp.where(is_even(), high_in[:, here], low_in[:, here]).astype(F32)
        low = lax.broadcasted_iota(jnp.int32, from_next.shape, 1) < pair
        next_swapped = swapped(from_next)
        third = jnp.where(low, from_next, next_swapped)
        fourth = jnp.where(low, next_swapped, from_next)
        start = jnp.where(low, from_prev, swapped(from_prev))
        place = jnp.broadcast_to(places[row : row + 1, :width], kv.shape)
        back = jnp.where(place == 2, third, jnp.where(place == 3, fourth, 0.0))
        back = jnp.where(place == 0, start, back)
        at = h * (width + pair)
        out[:, at : at + width] = (kv[...] + back).astype(BF16)
        query_back = head_of(from_prev, 2)
        query_back = jnp.concatenate([query_back, query_back], axis=1)
        place = places[2:3, row * pair : (row + 1) * pair]
        place = jnp.broadcast_to(place, query_back.shape)
        mine = dq[:, row * pair : (row + 1) * pair].astype(F32)
        total = mine + jnp.where(place == 0, query_back, 0.0)
        out[:, at + width : at + width + pair] = total.astype(BF16)


def input_part(packs, w_ref):
    parts = []
    for h in range(2):
        pack = packs[:, h * 6 * HEAD_WIDTH : (h + 1) * 6 * HEAD_WIDTH]
        values = jnp.concatenate([head_of(pack, 1), head_of(pack, 3)], axis=0)
        queries = jnp.concatenate([head_of(pack, 4), head_of(pack, 5)], axis=0)
        parts.append(dot(queries, w_ref[2 * h], ((1,), (1,))))
        parts.append(dot(values, w_ref[2 * h + 1], ((1,), (1,))))
    return sum(parts)


def peer_totals_kernel(
    places, kv_first, kv_second, dq_first, dq_second, high_in, low_in, send
):
    put_totals(1, places, (kv_first, kv_second), (dq_first, dq_second), high_in, low_in, send)


def own_totals_kernel(
    places, kv_first, kv_second, dq_first, dq_second, ap_keep, w_ref, send, high_in, low_in,
    keep, part, peer_part, ap_sum,
):
    ap_sum[...] = (ap_keep[...] + low_in[:, 8 * HEAD_WIDTH :].astype(F32)).astype(BF16)
    put_totals(0, places, (kv_first, kv_second), (dq_first, dq_second), high_in, low_in, keep)
    part[...] = input_part(keep, w_ref)
    peer_part[...] = input_part(send, w_ref).astype(BF16)


def all_heads(mine, theirs):
    upper = is_upper()
    mine, theirs = ([values.astype(F32) for values in side] for side in (mine, theirs))
    lower_heads = [jnp.where(upper, b, a) for a, b in zip(mine, theirs)]
    return lower_heads + [jnp.where(upper, a, b) for a, b in zip(mine, theirs)]


def heads_beside(packs, i):
    return jnp.concatenate([head_of(values, i) for values in packs], axis=1)


def grads_out_kernel(keep, recv, grad_query, grad_key, grad_value, done):
    stretch_len = keep.shape[0]
    wide = 6 * HEAD_WIDTH
    every = [slice(h * wide, (h + 1) * wide) for h in range(2)]
    packs = all_heads([keep[:, here] for here in every], [recv[:, here] for here in every])
    for s in range(STRETCHES_DEV):
        here = slice(s * stretch_len, (s + 1) * stretch_len)
        grad_key[here, :] = heads_beside(packs, 2 * s).astype(BF16)
        grad_value[here, :] = heads_beside(packs, 2 * s + 1).astype(BF16)
        grad_query[here, :] = heads_beside(packs, 4 + s).astype(BF16)
    done[...] = jnp.zeros(done.shape, done.dtype)


def adapter_out_kernel(own, peer_other, other, peer_own, input_sum, awaited, out, grad_input):
    even = is_even()
    rows = out.shape[1] // 2
    grad_input[...] = input_sum[...].astype(BF16)
    own, other, peer_own, peer_other = (
        ref[...].astype(F32) for ref in (own, other, peer_own, peer_other)
    )
    packs = all_heads(
        (jnp.where(even, own, other), jnp.where(even, other, own)),
        (jnp.where(even, peer_own, peer_other), jnp.where(even, peer_other, peer_own)),
    )
    for w in range(2):
        for i in range(2):
            out[w, i * rows : (i + 1) * rows, :] = heads_beside(packs, 2 * i + w)


def body(
    query_base, key_base, value_base, adapter_activation, adapter_up_weight, output_grad,
    stretch_doc, doc_first, slot_stretch,
):
    row_count, columns = query_base.shape
    rank = adapter_activation.shape[1]
    stretch_len = row_count // STRETCHES_DEV
    width = 4 * HEAD_WIDTH
    ctx_count = lax.axis_size("ctx")
    tp_count = lax.axis_size("tp")
    groups = ctx_count // GROUP_SIZE
    shape = jax.ShapeDtypeStruct

    def exchanged(array, flip):
        return lax.ppermute(array, "ctx", [(i, i ^ flip) for i in range(ctx_count)])

    def with_odd_pairs(array):
        pairs = []
        for i in range(ctx_count):
            group = i // GROUP_SIZE
            other = group + 1 if group % 2 else group - 1
            for t in range(tp_count):
                to = (i, t ^ 1)
                if 0 <= other < groups:
                    to = (other * GROUP_SIZE + i % GROUP_SIZE, t)
                pairs.append((i * tp_count + t, to[0] * tp_count + to[1]))
        return lax.ppermute(array, ("ctx", "tp"), pairs)

    def first_pack(*args):
        anywhere = pl.BlockSpec(memory_space=pl.ANY)
        return pl.pallas_call(
            first_kernel,
            out_shape=shape((STRETCHES_DEV, stretch_len, width + rank), BF16),
            in_specs=[anywhere] * len(args),
            out_specs=pl.BlockSpec(memory_space=pltpu.VMEM),
            scratch_shapes=[pltpu.VMEM(a.shape, a.dtype) for a in args]
            + [pltpu.SemaphoreType.DMA((len(args),))],
        )(*args)

    arrays = (
        key_base, value_base, query_base, output_grad, adapter_activation, adapter_up_weight
    )
    peer_first = exchanged(first_pack(*arrays), 1)
    pack_first = shape((STRETCHES_DEV, stretch_len, width + rank), BF16)
    pack_second = shape((STRETCHES_DEV, stretch_len, width), BF16)
    outs = [
        pack_second,
        pack_first,
        pack_second,
        shape((4, rank, HEAD_WIDTH), BF16),
        shape((3 + GROUP_STRETCHES, width + rank), jnp.int32),
        shape((GROUP_STRETCHES + 3, (GROUP_STRETCHES + 1) * stretch_len), jnp.int32),
    ]
    sent, own_first, own_second, w_heads, places, limits = call(
        functools.partial(rest_kernel, ctx_count), outs, 3
    )(stretch_doc, doc_first, slot_stretch, *arrays)

    peer_second = exchanged(sent, 1)
    edge = shape((stretch_len, width + 2 * rank), BF16)
    low_sent, high_sent = call(edge_kernel, [edge] * 2)(places, own_first, peer_first)
    high_first = with_odd_pairs(high_sent)
    low_first = exchanged(low_sent, GROUP_SIZE)
    edge = shape((stretch_len, width), BF16)
    low_sent, high_sent = call(edge_kernel, [edge] * 2)(places, own_second, peer_second)
    high_second = with_odd_pairs(high_sent)
    low_second = exchanged(low_sent, GROUP_SIZE)

    wide, low = shape((stretch_len, width), F32), shape((stretch_len, width), BF16)
    outs = [wide, wide, low, low, low, wide]
    act_rows = (GROUP_STRETCHES + 3) * stretch_len
    act, kv_own_first, kv_peer_first, dq_first, low_back, high_back, ap_first = call(
        functools.partial(attend_kernel, 0), [shape((act_rows, rank), BF16)] + outs
    )(limits, own_first, peer_first, low_first, high_first)
    outs = [wide, wide, low, shape((stretch_len, 3 * width), BF16)]
    outs += [shape((stretch_len, 2 * width), BF16), wide]
    kv_own_second, kv_peer_second, dq_second, low_back, high_back, ap_keep = call(
        functools.partial(attend_kernel, 1), outs
    )(
        limits, own_second, peer_second, low_second, high_second,
        act, low_back, high_back, ap_first,
    )
    low_back = exchanged(low_back, GROUP_SIZE)
    high_back = with_odd_pairs(high_back)

    back = shape((stretch_len, 2 * (width + 2 * HEAD_WIDTH)), BF16)
    (send,) = call(peer_totals_kernel, [back])(
        places, kv_peer_first, kv_peer_second, dq_first, dq_second, high_back, low_back
    )
    recv = exchanged(send, 1)
    part_dims = (row_count, rank)
    outs = [back, shape(part_dims, F32), shape(part_dims, BF16), low]
    keep, own_part, peer_part, total = call(own_totals_kernel, outs)(
        places, kv_own_first, kv_own_second, dq_first, dq_second, ap_keep, w_heads, send,
        high_back, low_back,
    )
    gi_recv = exchanged(peer_part, 1)

    flip = 2
    while flip < groups:
        theirs = exchanged(total, flip * GROUP_SIZE)
        total = (total.astype(F32) + theirs.astype(F32)).astype(BF16)
        flip *= 2
    peer_total = exchanged(total, 1)
    other = exchanged(total, GROUP_SIZE)
    peer_other = exchanged(total, GROUP_SIZE + 1)

    part = (own_part + gi_recv.astype(F32)).astype(BF16)
    sums = [part.astype(F32)]
    for by in range(1, tp_count):
        pairs = [(i, i ^ by) for i in range(tp_count)]
        sums.append(lax.ppermute(part, "tp", pairs).astype(F32))
    while len(sums) > 1:
        sums = [a + b for a, b in zip(sums[::2], sums[1::2])]

    outs = [shape((row_count, columns), BF16)] * 3 + [shape((8, 128), F32)]
    grad_query, grad_key, grad_value, done = call(grads_out_kernel, outs)(keep, recv)
    outs = [shape((2, rank, columns), F32), shape((row_count, rank), BF16)]
    grad_adapter, grad_input = call(adapter_out_kernel, outs)(
        total, peer_other, other, peer_total, sums[0], done
    )
    return (grad_query, grad_key, grad_value, grad_input, grad_adapter)


def solution(mesh):
    return jax.shard_map(
        body,
        mesh=mesh,
        in_specs=(
            P("ctx", "tp"),
            P("ctx", "tp"),
            P("ctx", "tp"),
            P("ctx", None),
            P(None, None, "tp"),
            P("ctx", "tp"),
            P(),
            P(),
            P(),
        ),
        out_specs=(
            P("ctx", "tp"),
            P("ctx", "tp"),
            P("ctx", "tp"),
            P("ctx", None),
            P(None, None, "tp"),
        ),
        check_vma=False,
    )
```

time: 213 us -> 53.8 us (0.25)
  waiting for transfers between devices: 112 us -> 20.9 us
  local copies, waits for them, and re-layouts: 21.2 us -> 0.04 us
  between operations: 17.7 us -> 0.85 us
  matrix products: 12.5 us -> 0 us
  blocking collectives: 11.2 us -> 0 us
  Pallas kernels: 0 us -> 11 us
  other arithmetic: 8.85 us -> 0.06 us
  starting transfers between devices: 27.7 us -> 20.8 us
    psum x1 -> x0, waiting for transfers between devices: 79.8 us -> none  [body(): grad_adapter = lax.psum(adapter_part, 'ctx')]
    dot_general x20 -> x0, matrix products: 12.5 us -> none  [the longest x2 4.73 us: add_values(): jnp.einsum('hqk,khe->qhe', probs_low, split_heads(pair[1]), preferred_ele...]
    psum x1 -> x0, blocking collectives: 11.2 us -> none  [body(): grad_input = lax.psum(input_part, 'tp').astype(jnp.bfloat16)]
    ppermute x8 -> x17, waiting for transfers between devices: 32.1 us -> 20.9 us  [the longest x11 19.4 us: exchanged(): return lax.ppermute(array, 'ctx', [(i, i ^ flip) for i in range(ctx_count)])]
    pallas_call x0 -> x10, Pallas kernels: none -> 11 us  [the longest x9 8.39 us: run(): pl.pallas_call(kernel, out_shape=outs, in_specs=specs, out_specs=[pl.Bloc...]
    ppermute x8 -> x17, starting transfers between devices: 27.7 us -> 20.8 us  [the longest x11 18.9 us: exchanged(): return lax.ppermute(array, 'ctx', [(i, i ^ flip) for i in range(ctx_count)])]
    cond x10 -> x0, local copies, waits for them, and re-layouts: 6.48 us -> none  [the longest x5 5.21 us: body(): lax.cond(useful, piece_grads, skip_piece, query_gradient)]
    unnamed x39 -> x18, local copies, waits for them, and re-layouts: 6.4 us -> 0.04 us
  transfers between devices with their start and end apart: 9 -> 17, of which waited for: 5 -> 9; matrix products, arithmetic and copies ran while one was open for 4% -> 0% of each run, Pallas kernels for 0% -> 8%
where the time goes in v1:
time: 53.8 us; the launch traced here: 53.6 us
  waiting for transfers between devices  20.9 us (39%)
  starting transfers between devices  20.8 us (39%)
  Pallas kernels  11 us (20%)
  between operations  0.85 us (2%)
    ppermute x11, waiting for transfers between devices, exchanged(): return lax.ppermute(array, 'ctx', [(i, i ^ flip) for i in range(ctx_count)])  19.4 us
    ppermute x11, starting transfers between devices, exchanged(): return lax.ppermute(array, 'ctx', [(i, i ^ flip) for i in range(ctx_count)])  18.9 us
    pallas_call x9, Pallas kernels, run(): pl.pallas_call(kernel, out_shape=outs, in_specs=specs, out_specs=[pl.Bloc...  8.39 us
    pallas_call x1, Pallas kernels, first_pack(): pl.pallas_call(first_kernel, out_shape=shape((STRETCHES_DEV, stretch_len,...  2.6 us
    ppermute x3, starting transfers between devices, body(): sums.append(lax.ppermute(part, 'tp', pairs).astype(F32))  1.92 us
    ppermute x3, waiting for transfers between devices, with_odd_pairs(): return lax.ppermute(array, ('ctx', 'tp'), pairs)  1.49 us
  transfers between devices with their start and end apart: 17, of which 9 were waited for; matrix products, arithmetic and copies ran while one was open for 0% of the time, Pallas kernels for 8%

profile of v1, /device:TPU:0, one launch (start us, length us, event | category | flops | bytes accessed | tf_op | source)
XLA Modules:
  0.0 53.6 jit_solution(1072063508449861299)
XLA Ops:
  0.7 2.6 %shard_map.129 = bf16[2,64,1024]{2,1,0:T(8,128)(2,1)} custom-call(bf16[128,896]{1,0:T(8,128)(2,1)} %k_hbm.1, bf16[128,896]{1,0:T(8,128)(2,1)} %v_hbm.1, bf16[128,896]{1,0:T(8,128)(2,1)} %q_hbm.1, bf16[128,896]{1,0:T(8,128)(2,1)} %g_hbm.1, bf16[128,128]{1,0:T(8,128)(2,1)} %a_hbm.1, bf16[2,128,896]{2,1,0:T(8,128)(2,1)} %w_hbm.1), custom_call_target="tpu_custom_call" | custom-call | tf_op jit(solution)/shard_map/pallas_call | solution.py:395
  3.3 3.0 %collective-permute-start = (bf16[2,64,1024]{2,1,0:T(8,128)(2,1)}, bf16[2,64,1024]{2,1,0:T(8,128)(2,1)S(1)}, u32[]{:S(2)}, u32[]{:S(2)}) collective-permute-start(bf16[2,64,1024]{2,1,0:T(8,128)(2,1)} %shard_map.129), channel_id=1, source_target_pairs={{0,4},{4,0},{8,12},{12,8},{16,20},{20,16},{24,28},{28,24},{1,5},{5... | collective-permute-start | bytes 786440 | tf_op jit(solution)/shard_map/ppermute | solution.py:379
  6.4 1.4 %shard_map.128 = (bf16[2,64,896]{2,1,0:T(8,128)(2,1)S(1)}, bf16[2,64,1024]{2,1,0:T(8,128)(2,1)S(1)}, bf16[2,64,896]{2,1,0:T(8,128)(2,1)S(1)}, bf16[4,128,224]{2,...) custom-call(s32[16]{0:T(128)S(1)} %copy-done.6, s32[16]{0:T(128)S(1)} %copy-done.7, s32[16]{0:T(128)S(1)} %copy-done.8, ...), custom_call_target="tpu_custom_call" | custom-call | bytes 2397120 | tf_op jit(solution)/shard_map/pallas_call | solution.py:36
  7.8 0.1 collective-permute-start.3
  7.9 5.8 %collective-permute-done.peer = bf16[2,64,1024]{2,1,0:T(8,128)(2,1)S(1)} collective-permute-done((bf16[2,64,1024]{2,1,0:T(8,128)(2,1)}, bf16[2,64,1024]{2,1,0:T(8,128)(2,1)S(1)}, u32[]{:S(2)}, u32[]{:S(2)}) %collective-permute-start) | collective-permute-done | bytes 262176 | tf_op jit(solution)/shard_map/ppermute | solution.py:379
  13.7 0.2 shard_map.130
  13.9 2.2 %collective-permute-start.1 = (bf16[64,1152]{1,0:T(8,128)(2,1)S(1)}, bf16[64,1152]{1,0:T(8,128)(2,1)S(1)}, u32[]{:S(2)}, u32[]{:S(2)}) collective-permute-start(bf16[64,1152]{1,0:T(8,128)(2,1)S(1)} %get-tuple-element.41), channel_id=1, source_target_pairs={{0,8},{4,12},{8,0},{12,4},{16,24},{20,28},{24,16},{28,20},{1,9},{5... | collective-permute-start | bytes 442376 | tf_op jit(solution)/shard_map/ppermute | solution.py:379
  16.1 1.7 %collective-permute-done.3.peer = bf16[2,64,896]{2,1,0:T(8,128)(2,1)S(1)} collective-permute-done((bf16[2,64,896]{2,1,0:T(8,128)(2,1)S(1)}, bf16[2,64,896]{2,1,0:T(8,128)(2,1)S(1)}, u32[]{:S(2)}, u32[]{:S(2)}) %collective-permute-start.3) | collective-permute-done | bytes 229408 | tf_op jit(solution)/shard_map/ppermute | solution.py:379
  17.8 0.2 shard_map.132
  18.0 1.9 %collective-permute-start.4 = (bf16[64,896]{1,0:T(8,128)(2,1)S(1)}, bf16[64,896]{1,0:T(8,128)(2,1)S(1)}, u32[]{:S(2)}, u32[]{:S(2)}) collective-permute-start(bf16[64,896]{1,0:T(8,128)(2,1)S(1)} %get-tuple-element.46), channel_id=1, source_target_pairs={{0,8},{4,12},{8,0},{12,4},{16,24},{20,28},{24,16},{28,20},{1,9},{5... | collective-permute-start | bytes 344072 | tf_op jit(solution)/shard_map/ppermute | solution.py:379
  19.8 1.6 %shard_map.131 = (bf16[448,128]{1,0:T(8,128)(2,1)S(1)}, f32[64,896]{1,0:T(8,128)S(1)}, f32[64,896]{1,0:T(8,128)S(1)}, bf16[64,896]{1,0:T(8,128)(2,1)S(1)}, bf16[...) custom-call(s32[7,320]{1,0:T(8,128)S(1)} %get-tuple-element.39.limits, ...), custom_call_target="tpu_custom_call" | custom-call | bytes 1975040 | tf_op jit(solution)/shard_map/pallas_call | solution.py:36
  21.4 1.4 %collective-permute-done.4.low_in = bf16[64,896]{1,0:T(8,128)(2,1)S(1)} collective-permute-done((bf16[64,896]{1,0:T(8,128)(2,1)S(1)}, bf16[64,896]{1,0:T(8,128)(2,1)S(1)}, u32[]{:S(2)}, u32[]{:S(2)}) %collective-permute-start.4) | collective-permute-done | bytes 114720 | tf_op jit(solution)/shard_map/ppermute | solution.py:379
  22.8 1.6 %shard_map.133 = (f32[64,896]{1,0:T(8,128)S(1)}, f32[64,896]{1,0:T(8,128)S(1)}, bf16[64,896]{1,0:T(8,128)(2,1)S(1)}, bf16[64,2688]{1,0:T(8,128)(2,1)S(1)}, bf16[...) custom-call(s32[7,320]{1,0:T(8,128)S(1)} %get-tuple-element.39.limits, bf16[2,64,896]{2,1,0:T(8,128)(2,1)S(1)} %get-tuple-element.44.own, ...), custom_call_target="tpu_custom_call" | custom-call | bytes 2646784 | tf_op jit(solution)/shard_map/pallas_call | solution.py:36
  24.4 3.0 %collective-permute-start.7 = (bf16[64,2688]{1,0:T(8,128)(2,1)S(1)}, bf16[64,2688]{1,0:T(8,128)(2,1)S(1)}, u32[]{:S(2)}, u32[]{:S(2)}) collective-permute-start(bf16[64,2688]{1,0:T(8,128)(2,1)S(1)} %get-tuple-element.60), channel_id=1, source_target_pairs={{0,8},{4,12},{8,0},{12,4},{16,24},{20,28},{24,16},{28,20},{1,9},{5... | collective-permute-start | bytes 1032200 | tf_op jit(solution)/shard_map/ppermute | solution.py:379
  27.4 1.5 %collective-permute-done.6.high_in = bf16[64,1792]{1,0:T(8,128)(2,1)S(1)} collective-permute-done((bf16[64,1792]{1,0:T(8,128)(2,1)S(1)}, bf16[64,1792]{1,0:T(8,128)(2,1)S(1)}, u32[]{:S(2)}, u32[]{:S(2)}) %collective-permute-start.6) | collective-permute-done | bytes 229408 | tf_op jit(solution)/shard_map/ppermute | solution.py:391
  28.9 4.8 %collective-permute-done.7.low_in = bf16[64,2688]{1,0:T(8,128)(2,1)S(1)} collective-permute-done((bf16[64,2688]{1,0:T(8,128)(2,1)S(1)}, bf16[64,2688]{1,0:T(8,128)(2,1)S(1)}, u32[]{:S(2)}, u32[]{:S(2)}) %collective-permute-start.7) | collective-permute-done | bytes 344096 | tf_op jit(solution)/shard_map/ppermute | solution.py:379
  33.7 0.5 shard_map.134.send
  34.2 0.7 %shard_map.135 = (bf16[64,2688]{1,0:T(8,128)(2,1)S(1)}, f32[128,128]{1,0:T(8,128)S(1)}, bf16[128,128]{1,0:T(8,128)(2,1)S(1)}, bf16[64,896]{1,0:T(8,128)(2,1)S(1)}) custom-call(s32[7,1024]{1,0:T(8,128)S(1)} %get-tuple-element.38.places, f32[64,896]{1,0:T(8,128)S(1)} %get-tuple-element.43.kv_first, f32[64,896]{1,0:T(8,128)S(1)} %get-tuple-element.52.kv_second, ...), custom_call_target="tpu_custom_call" | custom-call | bytes 2650112 | tf_op jit(solution)/shard_map/pallas_call | solution.py:36
  34.9 1.6 %collective-permute-start.13 = (bf16[128,128]{1,0:T(8,128)(2,1)S(1)}, bf16[128,128]{1,0:T(8,128)(2,1)S(1)}, u32[]{:S(2)}, u32[]{:S(2)}) collective-permute-start(bf16[128,128]{1,0:T(8,128)(2,1)S(1)} %get-tuple-element.67), channel_id=1, source_target_pairs={{0,4},{4,0},{8,12},{12,8},{16,20},{20,16},{24,28},{28,24},{1,5},{5... | collective-permute-start | bytes 98312 | tf_op jit(solution)/shard_map/ppermute | solution.py:379
  36.5 0.5 collective-permute-start.8
  37.0 3.0 %collective-permute-start.9 = (bf16[64,896]{1,0:T(8,128)(2,1)S(1)}, bf16[64,896]{1,0:T(8,128)(2,1)S(1)}, u32[]{:S(2)}, u32[]{:S(2)}) collective-permute-start(bf16[64,896]{1,0:T(8,128)(2,1)S(1)} %get-tuple-element.65), channel_id=1, source_target_pairs={{0,16},{4,20},{8,24},{12,28},{16,0},{20,4},{24,8},{28,12},{1,17},{... | collective-permute-start | bytes 344072 | tf_op jit(solution)/shard_map/ppermute | solution.py:379
  40.2 1.5 %collective-permute-start.15 = (bf16[128,128]{1,0:T(8,128)(2,1)S(1)}, bf16[128,128]{1,0:T(8,128)(2,1)S(1)}, u32[]{:S(2)}, u32[]{:S(2)}) collective-permute-start(bf16[128,128]{1,0:T(8,128)(2,1)S(1)} %add_convert_fusion.1), channel_id=1, source_target_pairs={{0,2},{1,3},{2,0},{3,1},{4,6},{5,7},{6,4},{7,5},{8,10},{9,11},{10,... | collective-permute-start | bytes 98312 | tf_op jit(solution)/shard_map/ppermute | solution.py:475
  41.7 0.3 collective-permute-start.14
  42.0 2.1 %collective-permute-done.9 = bf16[64,896]{1,0:T(8,128)(2,1)S(1)} collective-permute-done((bf16[64,896]{1,0:T(8,128)(2,1)S(1)}, bf16[64,896]{1,0:T(8,128)(2,1)S(1)}, u32[]{:S(2)}, u32[]{:S(2)}) %collective-permute-start.9) | collective-permute-done | bytes 114720 | tf_op jit(solution)/shard_map/ppermute | solution.py:379
  44.1 1.6 %collective-permute-start.12 = (bf16[64,896]{1,0:T(8,128)(2,1)S(1)}, bf16[64,896]{1,0:T(8,128)(2,1)S(1)}, u32[]{:S(2)}, u32[]{:S(2)}) collective-permute-start(bf16[64,896]{1,0:T(8,128)(2,1)S(1)} %add_convert_fusion.own), channel_id=1, source_target_pairs={{0,4},{4,0},{8,12},{12,8},{16,20},{20,16},{24,28},{28,24},{1,5},{5... | collective-permute-start | bytes 344072 | tf_op jit(solution)/shard_map/ppermute | solution.py:379
  45.7 0.5 collective-permute-start.11
  46.2 1.5 %collective-permute-start.10 = (bf16[64,896]{1,0:T(8,128)(2,1)S(1)}, bf16[64,896]{1,0:T(8,128)(2,1)S(1)}, u32[]{:S(2)}, u32[]{:S(2)}) collective-permute-start(bf16[64,896]{1,0:T(8,128)(2,1)S(1)} %add_convert_fusion.own), channel_id=1, source_target_pairs={{0,12},{4,8},{8,4},{12,0},{16,28},{20,24},{24,20},{28,16},{1,13},{... | collective-permute-start | bytes 344072 | tf_op jit(solution)/shard_map/ppermute | solution.py:379
  47.7 1.1 %shard_map.136 = (bf16[128,896]{1,0:T(8,128)(2,1)}, bf16[128,896]{1,0:T(8,128)(2,1)}, bf16[128,896]{1,0:T(8,128)(2,1)}, f32[8,128]{1,0:T(8,128)S(1)}) custom-call(bf16[64,2688]{1,0:T(8,128)(2,1)S(1)} %get-tuple-element.61.keep, bf16[64,2688]{1,0:T(8,128)(2,1)S(1)} %collective-permute-done.8.recv), custom_call_target="tpu_custom_call" | custom-call | bytes 1380352 | tf_op jit(solution)/shard_map/pallas_call | solution.py:36
  48.8 0.9 %collective-permute-done.12.peer_own = bf16[64,896]{1,0:T(8,128)(2,1)S(1)} collective-permute-done((bf16[64,896]{1,0:T(8,128)(2,1)S(1)}, bf16[64,896]{1,0:T(8,128)(2,1)S(1)}, u32[]{:S(2)}, u32[]{:S(2)}) %collective-permute-start.12) | collective-permute-done | bytes 114720 | tf_op jit(solution)/shard_map/ppermute | solution.py:379
  49.7 0.9 %collective-permute-done.11.other = bf16[64,896]{1,0:T(8,128)(2,1)S(1)} collective-permute-done((bf16[64,896]{1,0:T(8,128)(2,1)S(1)}, bf16[64,896]{1,0:T(8,128)(2,1)S(1)}, u32[]{:S(2)}, u32[]{:S(2)}) %collective-permute-start.11) | collective-permute-done | bytes 114720 | tf_op jit(solution)/shard_map/ppermute | solution.py:379
  50.6 1.8 %collective-permute-done.10.peer_other = bf16[64,896]{1,0:T(8,128)(2,1)S(1)} collective-permute-done((bf16[64,896]{1,0:T(8,128)(2,1)S(1)}, bf16[64,896]{1,0:T(8,128)(2,1)S(1)}, u32[]{:S(2)}, u32[]{:S(2)}) %collective-permute-start.10) | collective-permute-done | bytes 114720 | tf_op jit(solution)/shard_map/ppermute | solution.py:379
  52.4 1.2 %shard_map.137 = (f32[2,128,896]{2,1,0:T(8,128)}, bf16[128,128]{1,0:T(8,128)(2,1)}) custom-call(bf16[64,896]{1,0:T(8,128)(2,1)S(1)} %add_convert_fusion.own, bf16[64,896]{1,0:T(8,128)(2,1)S(1)} %collective-permute-done.10.peer_other, bf16[64,896]{1,0:T(8,128)(2,1)S(1)} %collective-permute-done.11.other, ...), custom_call_target="tpu_custom_call" | custom-call | bytes 1478656 | tf_op jit(solution)/shard_map/pallas_call | solution.py:36
  (33 shorter events, 0.2 us)
Async XLA Ops:
  0.6 5.7 %copy-start.4 = (bf16[128,896]{1,0:T(8,128)(2,1)S(1)}, bf16[128,896]{1,0:T(8,128)(2,1)}, u32[]{:S(2)}) copy-start(bf16[128,896]{1,0:T(8,128)(2,1)} %g_hbm.1) | copy-start | bytes 688132
  0.6 5.7 %copy-start = (bf16[2,128,896]{2,1,0:T(8,128)(2,1)S(1)}, bf16[2,128,896]{2,1,0:T(8,128)(2,1)}, u32[]{:S(2)}) copy-start(bf16[2,128,896]{2,1,0:T(8,128)(2,1)} %w_hbm.1) | copy-start | bytes 1376260
  0.7 5.7 %copy-start.5 = (bf16[128,128]{1,0:T(8,128)(2,1)S(1)}, bf16[128,128]{1,0:T(8,128)(2,1)}, u32[]{:S(2)}) copy-start(bf16[128,128]{1,0:T(8,128)(2,1)} %a_hbm.1) | copy-start | bytes 98308
  0.7 5.7 %copy-start.2 = (bf16[128,896]{1,0:T(8,128)(2,1)S(1)}, bf16[128,896]{1,0:T(8,128)(2,1)}, u32[]{:S(2)}) copy-start(bf16[128,896]{1,0:T(8,128)(2,1)} %v_hbm.1) | copy-start | bytes 688132
  0.7 5.7 %copy-start.1 = (bf16[128,896]{1,0:T(8,128)(2,1)S(1)}, bf16[128,896]{1,0:T(8,128)(2,1)}, u32[]{:S(2)}) copy-start(bf16[128,896]{1,0:T(8,128)(2,1)} %k_hbm.1) | copy-start | bytes 688132
  0.7 5.7 %copy-start.3 = (bf16[128,896]{1,0:T(8,128)(2,1)S(1)}, bf16[128,896]{1,0:T(8,128)(2,1)}, u32[]{:S(2)}) copy-start(bf16[128,896]{1,0:T(8,128)(2,1)} %q_hbm.1) | copy-start | bytes 688132
  0.7 5.7 %copy-start.8 = (s32[16]{0:T(128)S(1)}, s32[16]{0:T(128)}, u32[]{:S(2)}) copy-start(s32[16]{0:T(128)} %slot.1) | copy-start | bytes 196
  0.7 5.7 %copy-start.7 = (s32[16]{0:T(128)S(1)}, s32[16]{0:T(128)}, u32[]{:S(2)}) copy-start(s32[16]{0:T(128)} %first.1) | copy-start | bytes 196
  0.7 5.7 %copy-start.6 = (s32[16]{0:T(128)S(1)}, s32[16]{0:T(128)}, u32[]{:S(2)}) copy-start(s32[16]{0:T(128)} %doc.1) | copy-start | bytes 196
  3.3 10.4 %collective-permute-start = (bf16[2,64,1024]{2,1,0:T(8,128)(2,1)}, bf16[2,64,1024]{2,1,0:T(8,128)(2,1)S(1)}, u32[]{:S(2)}, u32[]{:S(2)}) collective-permute-start(bf16[2,64,1024]{2,1,0:T(8,128)(2,1)} %shard_map.129), channel_id=1, source_target_pairs={{0,4},{4,0},{8,12},{12,8},{16,20},{20,16},{24,28},{28,24},{1,5},{5... | collective-permute-start | bytes 786440 | tf_op jit(solution)/shard_map/ppermute | solution.py:379
  7.8 10.0 %collective-permute-start.3 = (bf16[2,64,896]{2,1,0:T(8,128)(2,1)S(1)}, bf16[2,64,896]{2,1,0:T(8,128)(2,1)S(1)}, u32[]{:S(2)}, u32[]{:S(2)}) collective-permute-start(bf16[2,64,896]{2,1,0:T(8,128)(2,1)S(1)} %get-tuple-element.45), channel_id=1, source_target_pairs={{0,4},{4,0},{8,12},{12,8},{16,20},{20,16},{24,28},{28,24},{1,5},{5... | collective-permute-start | bytes 688136 | tf_op jit(solution)/shard_map/ppermute | solution.py:379
  13.9 5.9 %collective-permute-start.1 = (bf16[64,1152]{1,0:T(8,128)(2,1)S(1)}, bf16[64,1152]{1,0:T(8,128)(2,1)S(1)}, u32[]{:S(2)}, u32[]{:S(2)}) collective-permute-start(bf16[64,1152]{1,0:T(8,128)(2,1)S(1)} %get-tuple-element.41), channel_id=1, source_target_pairs={{0,8},{4,12},{8,0},{12,4},{16,24},{20,28},{24,16},{28,20},{1,9},{5... | collective-permute-start | bytes 442376 | tf_op jit(solution)/shard_map/ppermute | solution.py:379
  16.1 3.8 %collective-permute-start.2 = (bf16[64,1152]{1,0:T(8,128)(2,1)S(1)}, bf16[64,1152]{1,0:T(8,128)(2,1)S(1)}, u32[]{:S(2)}, u32[]{:S(2)}) collective-permute-start(bf16[64,1152]{1,0:T(8,128)(2,1)S(1)} %get-tuple-element.42), channel_id=1, source_target_pairs={{0,1},{1,0},{2,3},{3,2},{4,5},{5,4},{6,7},{7,6},{8,16},{9,17},{10,... | collective-permute-start | bytes 442376 | tf_op jit(solution)/shard_map/ppermute | solution.py:391
  18.0 4.9 %collective-permute-start.4 = (bf16[64,896]{1,0:T(8,128)(2,1)S(1)}, bf16[64,896]{1,0:T(8,128)(2,1)S(1)}, u32[]{:S(2)}, u32[]{:S(2)}) collective-permute-start(bf16[64,896]{1,0:T(8,128)(2,1)S(1)} %get-tuple-element.46), channel_id=1, source_target_pairs={{0,8},{4,12},{8,0},{12,4},{16,24},{20,28},{24,16},{28,20},{1,9},{5... | collective-permute-start | bytes 344072 | tf_op jit(solution)/shard_map/ppermute | solution.py:379
  19.8 3.0 %collective-permute-start.5 = (bf16[64,896]{1,0:T(8,128)(2,1)S(1)}, bf16[64,896]{1,0:T(8,128)(2,1)S(1)}, u32[]{:S(2)}, u32[]{:S(2)}) collective-permute-start(bf16[64,896]{1,0:T(8,128)(2,1)S(1)} %get-tuple-element.47), channel_id=1, source_target_pairs={{0,1},{1,0},{2,3},{3,2},{4,5},{5,4},{6,7},{7,6},{8,16},{9,17},{10,... | collective-permute-start | bytes 344072 | tf_op jit(solution)/shard_map/ppermute | solution.py:391
  24.4 9.3 %collective-permute-start.7 = (bf16[64,2688]{1,0:T(8,128)(2,1)S(1)}, bf16[64,2688]{1,0:T(8,128)(2,1)S(1)}, u32[]{:S(2)}, u32[]{:S(2)}) collective-permute-start(bf16[64,2688]{1,0:T(8,128)(2,1)S(1)} %get-tuple-element.60), channel_id=1, source_target_pairs={{0,8},{4,12},{8,0},{12,4},{16,24},{20,28},{24,16},{28,20},{1,9},{5... | collective-permute-start | bytes 1032200 | tf_op jit(solution)/shard_map/ppermute | solution.py:379
  27.4 1.5 %collective-permute-start.6 = (bf16[64,1792]{1,0:T(8,128)(2,1)S(1)}, bf16[64,1792]{1,0:T(8,128)(2,1)S(1)}, u32[]{:S(2)}, u32[]{:S(2)}) collective-permute-start(bf16[64,1792]{1,0:T(8,128)(2,1)S(1)} %get-tuple-element.59), channel_id=1, source_target_pairs={{0,1},{1,0},{2,3},{3,2},{4,5},{5,4},{6,7},{7,6},{8,16},{9,17},{10,... | collective-permute-start | bytes 688136 | tf_op jit(solution)/shard_map/ppermute | solution.py:391
  34.9 5.1 %collective-permute-start.13 = (bf16[128,128]{1,0:T(8,128)(2,1)S(1)}, bf16[128,128]{1,0:T(8,128)(2,1)S(1)}, u32[]{:S(2)}, u32[]{:S(2)}) collective-permute-start(bf16[128,128]{1,0:T(8,128)(2,1)S(1)} %get-tuple-element.67), channel_id=1, source_target_pairs={{0,4},{4,0},{8,12},{12,8},{16,20},{20,16},{24,28},{28,24},{1,5},{5... | collective-permute-start | bytes 98312 | tf_op jit(solution)/shard_map/ppermute | solution.py:379
  36.5 11.2 %collective-permute-start.8 = (bf16[64,2688]{1,0:T(8,128)(2,1)S(1)}, bf16[64,2688]{1,0:T(8,128)(2,1)S(1)}, u32[]{:S(2)}, u32[]{:S(2)}) collective-permute-start(bf16[64,2688]{1,0:T(8,128)(2,1)S(1)} %shard_map.134.send), channel_id=1, source_target_pairs={{0,4},{4,0},{8,12},{12,8},{16,20},{20,16},{24,28},{28,24},{1,5},{5... | collective-permute-start | bytes 1032200 | tf_op jit(solution)/shard_map/ppermute | solution.py:379
  37.0 7.0 %collective-permute-start.9 = (bf16[64,896]{1,0:T(8,128)(2,1)S(1)}, bf16[64,896]{1,0:T(8,128)(2,1)S(1)}, u32[]{:S(2)}, u32[]{:S(2)}) collective-permute-start(bf16[64,896]{1,0:T(8,128)(2,1)S(1)} %get-tuple-element.65), channel_id=1, source_target_pairs={{0,16},{4,20},{8,24},{12,28},{16,0},{20,4},{24,8},{28,12},{1,17},{... | collective-permute-start | bytes 344072 | tf_op jit(solution)/shard_map/ppermute | solution.py:379
  40.1 5.6 %collective-permute-start.16 = (bf16[128,128]{1,0:T(8,128)(2,1)S(1)}, bf16[128,128]{1,0:T(8,128)(2,1)S(1)}, u32[]{:S(2)}, u32[]{:S(2)}) collective-permute-start(bf16[128,128]{1,0:T(8,128)(2,1)S(1)} %add_convert_fusion.1), channel_id=1, source_target_pairs={{0,3},{1,2},{2,1},{3,0},{4,7},{5,6},{6,5},{7,4},{8,11},{9,10},{10,... | collective-permute-start | bytes 98312 | tf_op jit(solution)/shard_map/ppermute | solution.py:475
  40.2 6.0 %collective-permute-start.15 = (bf16[128,128]{1,0:T(8,128)(2,1)S(1)}, bf16[128,128]{1,0:T(8,128)(2,1)S(1)}, u32[]{:S(2)}, u32[]{:S(2)}) collective-permute-start(bf16[128,128]{1,0:T(8,128)(2,1)S(1)} %add_convert_fusion.1), channel_id=1, source_target_pairs={{0,2},{1,3},{2,0},{3,1},{4,6},{5,7},{6,4},{7,5},{8,10},{9,11},{10,... | collective-permute-start | bytes 98312 | tf_op jit(solution)/shard_map/ppermute | solution.py:475
  41.7 6.0 %collective-permute-start.14 = (bf16[128,128]{1,0:T(8,128)(2,1)S(1)}, bf16[128,128]{1,0:T(8,128)(2,1)S(1)}, u32[]{:S(2)}, u32[]{:S(2)}) collective-permute-start(bf16[128,128]{1,0:T(8,128)(2,1)S(1)} %add_convert_fusion.1), channel_id=1, source_target_pairs={{0,1},{1,0},{2,3},{3,2},{4,5},{5,4},{6,7},{7,6},{8,9},{9,8},{10,11... | collective-permute-start | bytes 98312 | tf_op jit(solution)/shard_map/ppermute | solution.py:475
  44.1 5.6 %collective-permute-start.12 = (bf16[64,896]{1,0:T(8,128)(2,1)S(1)}, bf16[64,896]{1,0:T(8,128)(2,1)S(1)}, u32[]{:S(2)}, u32[]{:S(2)}) collective-permute-start(bf16[64,896]{1,0:T(8,128)(2,1)S(1)} %add_convert_fusion.own), channel_id=1, source_target_pairs={{0,4},{4,0},{8,12},{12,8},{16,20},{20,16},{24,28},{28,24},{1,5},{5... | collective-permute-start | bytes 344072 | tf_op jit(solution)/shard_map/ppermute | solution.py:379
  45.7 4.9 %collective-permute-start.11 = (bf16[64,896]{1,0:T(8,128)(2,1)S(1)}, bf16[64,896]{1,0:T(8,128)(2,1)S(1)}, u32[]{:S(2)}, u32[]{:S(2)}) collective-permute-start(bf16[64,896]{1,0:T(8,128)(2,1)S(1)} %add_convert_fusion.own), channel_id=1, source_target_pairs={{0,8},{4,12},{8,0},{12,4},{16,24},{20,28},{24,16},{28,20},{1,9},{5... | collective-permute-start | bytes 344072 | tf_op jit(solution)/shard_map/ppermute | solution.py:379
  46.2 6.2 %collective-permute-start.10 = (bf16[64,896]{1,0:T(8,128)(2,1)S(1)}, bf16[64,896]{1,0:T(8,128)(2,1)S(1)}, u32[]{:S(2)}, u32[]{:S(2)}) collective-permute-start(bf16[64,896]{1,0:T(8,128)(2,1)S(1)} %add_convert_fusion.own), channel_id=1, source_target_pairs={{0,12},{4,8},{8,4},{12,0},{16,28},{20,24},{24,20},{28,16},{1,13},{... | collective-permute-start | bytes 344072 | tf_op jit(solution)/shard_map/ppermute | solution.py:379
